TPU v7x, 32 devices: a whole 2x2x4 slice. The times are simulated.
32 devices in a mesh: dp: 8 (over y, x, core), tensor: 4 (over z).
Axes of the slice: x: 2, y: 2, z: 4, core: 2. Of those that a mesh axis runs over, the one named last changes fastest.
Arguments:
- activations: bfloat16 [584, 16, 1024], P('tensor', 'dp'), may hold values from -6 to 6
- cotangent: bfloat16 [584, 16, 1024], P('tensor', 'dp'), may hold values from -6 to 6
- token_valid: int32 [16, 584], P('dp'), may hold values from 0 to 1, as said below
- image_counts: int32 [8], P('dp'), may hold values from 1 to 2, as said below
- pre_gain: bfloat16 [1024], P('dp'), may hold values from 0.5 to 1.5
- pre_shift: bfloat16 [1024], P('dp'), may hold values from -3 to 3
- attn_weight: bfloat16 [3, 1024, 1024], P(None, 'dp', 'tensor'), may hold values from -0.1875 to 0.1875
- attn_bias: bfloat16 [2, 1024], P(None, 'tensor'), may hold values from -3 to 3
- proj_weight: bfloat16 [1024, 1024], P('tensor', 'dp'), may hold values from -0.5 to 0.5
- proj_bias: bfloat16 [1024], P('dp'), may hold values from -3 to 3
- mid_gain: bfloat16 [1024], P('dp'), may hold values from 0.5 to 1.5
- mid_shift: bfloat16 [1024], P('dp'), may hold values from -3 to 3
- up_weight: bfloat16 [1024, 4096], P('dp', 'tensor'), may hold values from -0.1875 to 0.1875
- up_bias: bfloat16 [4096], P('tensor'), may hold values from -3 to 3
- down_weight: bfloat16 [4096, 1024], P('tensor', 'dp'), may hold values from -0.09375 to 0.09375
- down_bias: bfloat16 [1024], P('dp'), may hold values from -3 to 3
Outputs:
- block_out: bfloat16 [584, 16, 1024], P('tensor', 'dp')
- input_grad: float32 [584, 16, 1024], P('tensor', 'dp')
- pregain_grad: float32 [1024], P('dp')
- preshift_grad: float32 [1024], P('dp')
- attnweight_grad: float32 [3, 1024, 1024], P(None, 'dp', 'tensor')
- attnbias_grad: float32 [2, 1024], P(None, 'tensor')
- projweight_grad: float32 [1024, 1024], P('tensor', 'dp')
- projbias_grad: float32 [1024], P('dp')
- midgain_grad: float32 [1024], P('dp')
- midshift_grad: float32 [1024], P('dp')
- upweight_grad: float32 [1024, 4096], P('dp', 'tensor')
- upbias_grad: float32 [4096], P('tensor')
- downweight_grad: float32 [4096, 1024], P('tensor', 'dp')
- downbias_grad: float32 [1024], P('dp')
Inputs may be any that keep to these rules, and one draw needn't show every extreme that they name: `token_valid`: the valid tokens of each image are a leading run of 292 or more positions, followed only by padding. The slots of a dp index that hold images are its first image_counts ones; in every draw some dp index holds 2 images.
All inputs are finite; a program needn't handle non-finite values.
Results may differ from a plain program's by a relative error of at most 0.012.
Values may be sent and summed in bfloat16 or wider, within the bound.
A program may use at most 192 MiB of HBM per device.

v0:
```python
import jax
import jax.numpy as jnp
from jax import lax
from jax.sharding import PartitionSpec as P

D = 1024
H = 16
HD = 64
MB = 2
EPS = 1e-06
NEG = -1000000000.0


def layer_norm(values, gain, shift):
    center = values - jnp.mean(values, axis=-1, keepdims=True)
    spread = jnp.mean(center * center, axis=-1, keepdims=True)
    return center * lax.rsqrt(spread + EPS) * gain + shift


def gelu_exact(values):
    return jax.nn.gelu(values, approximate=False)


def per_device(
    activations,
    cotangent,
    token_valid,
    image_counts,
    pre_gain,
    pre_shift,
    attn_weight,
    attn_bias,
    proj_weight,
    proj_bias,
    mid_gain,
    mid_shift,
    up_weight,
    up_bias,
    down_weight,
    down_bias,
):
    f32 = jnp.float32
    bf16 = jnp.bfloat16
    tensor_size = lax.axis_size("tensor")
    local_rows = activations.shape[0]
    slots = activations.shape[1]
    per_micro = slots // MB
    heads_here = H // tensor_size
    width_here = attn_weight.shape[2]
    hidden_here = up_weight.shape[1]
    scale = HD ** (-0.5)
    first_row = lax.axis_index("tensor") * local_rows
    my_valid = lax.dynamic_slice_in_dim(token_valid, first_row, local_rows, 1).astype(f32)
    slot_live = (jnp.arange(slots, dtype=jnp.int32) < image_counts[0]).astype(f32)
    attn_bias_f = attn_bias.astype(f32)
    up_bias_f = up_bias.astype(f32)
    acc_attn = jnp.zeros((3, D, width_here), f32)
    acc_proj = jnp.zeros((width_here, D), f32)
    acc_up = jnp.zeros((D, hidden_here), f32)
    acc_down = jnp.zeros((hidden_here, D), f32)
    acc_attn_bias = jnp.zeros((2, width_here), f32)
    acc_up_bias = jnp.zeros((hidden_here,), f32)
    acc_vectors = [jnp.zeros((D,), f32) for unused in range(6)]
    block_parts = []
    input_parts = []
    for micro_step in range(MB):
        gathered = (
            lax.all_gather(attn_weight, "dp", axis=1, tiled=True),
            lax.all_gather(proj_weight, "dp", axis=1, tiled=True),
            lax.all_gather(up_weight, "dp", axis=0, tiled=True),
            lax.all_gather(down_weight, "dp", axis=1, tiled=True),
            lax.all_gather(pre_gain, "dp", axis=0, tiled=True),
            lax.all_gather(pre_shift, "dp", axis=0, tiled=True),
            lax.all_gather(proj_bias, "dp", axis=0, tiled=True),
            lax.all_gather(mid_gain, "dp", axis=0, tiled=True),
            lax.all_gather(mid_shift, "dp", axis=0, tiled=True),
            lax.all_gather(down_bias, "dp", axis=0, tiled=True),
        )
        qkv_full, proj_full, upw_full, downw_full = (
            gathered[0],
            gathered[1],
            gathered[2],
            gathered[3],
        )
        gain_one, shift_one, proj_bias_f, gain_two, shift_two, down_bias_f = [
            item.astype(f32) for item in gathered[4:]
        ]
        offset = micro_step * per_micro
        inputs_f = activations[:, offset : offset + per_micro].astype(f32)
        key_valid = token_valid[offset : offset + per_micro]
        key_bias = jnp.where(key_valid > 0, 0.0, NEG).astype(f32)
        out_mask = jnp.transpose(
            slot_live[offset : offset + per_micro][:, None] * my_valid[offset : offset + per_micro]
        )[:, :, None]
        normed = layer_norm(inputs_f, gain_one, shift_one).astype(bf16)
        normed_all = lax.all_gather(normed, "tensor", axis=0, tiled=True)
        full_rows = normed_all.shape[0]
        projected = jnp.einsum("sid,cde->csie", normed_all, qkv_full, preferred_element_type=f32)
        queries = (
            (projected[0] + attn_bias_f[0])
            .astype(bf16)
            .reshape(full_rows, per_micro, heads_here, HD)
        )
        keys = projected[1].astype(bf16).reshape(full_rows, per_micro, heads_here, HD)
        values = (
            (projected[2] + attn_bias_f[1])
            .astype(bf16)
            .reshape(full_rows, per_micro, heads_here, HD)
        )

        def scores_of(query_part, key_part):
            raw = jnp.einsum("qihe,kihe->ihqk", query_part, key_part, preferred_element_type=f32)
            return raw * scale + key_bias[:, None, None, :]

        scores = scores_of(queries, keys)
        top = jnp.max(scores, axis=-1, keepdims=True)
        expo = jnp.exp(scores - top)
        total = jnp.sum(expo, axis=-1, keepdims=True)
        logsum = top + jnp.log(total)
        probs_low = (expo / total).astype(bf16)
        attended = (
            jnp.einsum("ihqk,kihe->qihe", probs_low, values, preferred_element_type=f32)
            .astype(bf16)
            .reshape(full_rows, per_micro, width_here)
        )
        resid = (
            inputs_f
            + lax.psum_scatter(
                jnp.einsum("sie,ed->sid", attended, proj_full, preferred_element_type=f32),
                "tensor",
                scatter_dimension=0,
                tiled=True,
            )
            + proj_bias_f
        )
        normed2 = layer_norm(resid, gain_two, shift_two).astype(bf16)
        normed2_all = lax.all_gather(normed2, "tensor", axis=0, tiled=True)
        hidden_pre = (
            jnp.einsum("sid,df->sif", normed2_all, upw_full, preferred_element_type=f32) + up_bias_f
        )
        hidden = gelu_exact(hidden_pre).astype(bf16)
        mlp_out = (
            lax.psum_scatter(
                jnp.einsum("sif,fd->sid", hidden, downw_full, preferred_element_type=f32).astype(
                    jnp.bfloat16
                ),
                "tensor",
                scatter_dimension=0,
                tiled=True,
            ).astype(jnp.float32)
            + down_bias_f
        )
        block_parts.append(((resid + mlp_out) * out_mask).astype(bf16))
        outer = cotangent[:, offset : offset + per_micro].astype(f32) * out_mask
        mlp_grad = outer.astype(bf16)
        acc_vectors[5] = acc_vectors[5] + jnp.sum(mlp_grad.astype(f32), axis=(0, 1))
        mlp_grad_all = lax.all_gather(mlp_grad, "tensor", axis=0, tiled=True)
        acc_down = acc_down + jnp.einsum(
            "sif,sid->fd", hidden, mlp_grad_all, preferred_element_type=f32
        )
        hidden_grad = jnp.einsum(
            "sid,fd->sif", mlp_grad_all, downw_full, preferred_element_type=f32
        )
        unused, gelu_back = jax.vjp(gelu_exact, hidden_pre)
        pre_grad = gelu_back(hidden_grad)[0].astype(bf16)
        acc_up_bias = acc_up_bias + jnp.sum(pre_grad.astype(f32), axis=(0, 1))
        acc_up = acc_up + jnp.einsum(
            "sid,sif->df", normed2_all, pre_grad, preferred_element_type=f32
        )
        normed2_grad = lax.psum_scatter(
            jnp.einsum("sif,df->sid", pre_grad, upw_full, preferred_element_type=f32),
            "tensor",
            scatter_dimension=0,
            tiled=True,
        )
        unused, second_back = jax.vjp(layer_norm, resid, gain_two, shift_two)
        resid_part, gain_two_grad, shift_two_grad = second_back(normed2_grad)
        acc_vectors[3] = acc_vectors[3] + gain_two_grad
        acc_vectors[4] = acc_vectors[4] + shift_two_grad
        resid_grad = outer + resid_part
        branch_grad = resid_grad.astype(bf16)
        acc_vectors[2] = acc_vectors[2] + jnp.sum(branch_grad.astype(f32), axis=(0, 1))
        branch_all = lax.all_gather(branch_grad, "tensor", axis=0, tiled=True)
        acc_proj = acc_proj + jnp.einsum(
            "sie,sid->ed", attended, branch_all, preferred_element_type=f32
        )
        att_grad = (
            jnp.einsum("sid,ed->sie", branch_all, proj_full, preferred_element_type=f32)
            .astype(bf16)
            .reshape(full_rows, per_micro, heads_here, HD)
        )
        probs = jnp.exp(scores_of(queries, keys) - logsum)
        probs_again = probs.astype(bf16)
        value_grad = jnp.einsum(
            "ihqk,qihe->kihe", probs_again, att_grad, preferred_element_type=f32
        ).astype(bf16)
        prob_grad = jnp.einsum("qihe,kihe->ihqk", att_grad, values, preferred_element_type=f32)
        score_grad = (
            probs * (prob_grad - jnp.sum(prob_grad * probs, axis=-1, keepdims=True))
        ).astype(bf16)
        query_grad = (
            jnp.einsum("ihqk,kihe->qihe", score_grad, keys, preferred_element_type=f32) * scale
        ).astype(bf16)
        key_grad = (
            jnp.einsum("ihqk,qihe->kihe", score_grad, queries, preferred_element_type=f32) * scale
        ).astype(bf16)
        qkv_grad = jnp.stack([query_grad, key_grad, value_grad]).reshape(
            3, full_rows, per_micro, width_here
        )
        acc_attn_bias = acc_attn_bias + jnp.stack(
            [
                jnp.sum(qkv_grad[0].astype(f32), axis=(0, 1)),
                jnp.sum(qkv_grad[2].astype(f32), axis=(0, 1)),
            ]
        )
        acc_attn = acc_attn + jnp.einsum(
            "sid,csie->cde", normed_all, qkv_grad, preferred_element_type=f32
        )
        normed_grad = lax.psum_scatter(
            jnp.einsum("csie,cde->sid", qkv_grad, qkv_full, preferred_element_type=f32),
            "tensor",
            scatter_dimension=0,
            tiled=True,
        )
        unused, first_back = jax.vjp(layer_norm, inputs_f, gain_one, shift_one)
        input_part, gain_one_grad, shift_one_grad = first_back(normed_grad)
        acc_vectors[0] = acc_vectors[0] + gain_one_grad
        acc_vectors[1] = acc_vectors[1] + shift_one_grad
        input_parts.append(resid_grad + input_part)
    summed = lax.psum(
        (
            acc_vectors[0],
            acc_vectors[1],
            acc_vectors[2],
            acc_vectors[3],
            acc_vectors[4],
            acc_vectors[5],
        ),
        "tensor",
    )
    owned = (
        lax.psum_scatter(acc_attn, "dp", scatter_dimension=1, tiled=True),
        lax.psum_scatter(acc_proj, "dp", scatter_dimension=1, tiled=True),
        lax.psum_scatter(acc_up, "dp", scatter_dimension=0, tiled=True),
        lax.psum_scatter(acc_down, "dp", scatter_dimension=1, tiled=True),
        lax.psum_scatter(summed[0], "dp", scatter_dimension=0, tiled=True),
        lax.psum_scatter(summed[1], "dp", scatter_dimension=0, tiled=True),
        lax.psum_scatter(summed[2], "dp", scatter_dimension=0, tiled=True),
        lax.psum_scatter(summed[3], "dp", scatter_dimension=0, tiled=True),
        lax.psum_scatter(summed[4], "dp", scatter_dimension=0, tiled=True),
        lax.psum_scatter(summed[5], "dp", scatter_dimension=0, tiled=True),
    )
    bias_sums = lax.psum((acc_attn_bias, acc_up_bias), "dp")
    block_out = jnp.concatenate(block_parts, axis=1)
    input_grad = jnp.concatenate(input_parts, axis=1)
    return (
        block_out,
        input_grad,
        owned[4],
        owned[5],
        owned[0],
        bias_sums[0],
        owned[1],
        owned[6],
        owned[7],
        owned[8],
        owned[2],
        bias_sums[1],
        owned[3],
        owned[9],
    )


def solution(mesh):
    return jax.shard_map(
        per_device,
        mesh=mesh,
        in_specs=(
            P("tensor", "dp", None),
            P("tensor", "dp", None),
            P("dp", None),
            P("dp"),
            P("dp"),
            P("dp"),
            P(None, "dp", "tensor"),
            P(None, "tensor"),
            P("tensor", "dp"),
            P("dp"),
            P("dp"),
            P("dp"),
            P("dp", "tensor"),
            P("tensor"),
            P("tensor", "dp"),
            P("dp"),
        ),
        out_specs=(
            P("tensor", "dp", None),
            P("tensor", "dp", None),
            P("dp"),
            P("dp"),
            P(None, "dp", "tensor"),
            P(None, "tensor"),
            P("tensor", "dp"),
            P("dp"),
            P("dp"),
            P("dp"),
            P("dp", "tensor"),
            P("tensor"),
            P("tensor", "dp"),
            P("dp"),
        ),
        check_vma=False,
    )
```

profile of v0, /device:TPU:0, one launch (start us, length us, event | category | flops | bytes accessed | tf_op | source)
XLA Modules:
  0.0 1428.0 jit_solution(13615151279646853309)
XLA Ops:
  7.2 3.1 convert_reduce_fusion.11
  10.4 10.3 all-gather
  20.7 8.6 all-gather.1
  29.3 5.2 multiply_reduce_fusion.13
  39.6 9.6 all_gather.68
  49.2 40.0 %all-gather.28.cloned.1.call-done = bf16[584,1,1024]{2,1,0:T(2,128)(2,1)} async-done(((bf16[146,1,1024]{2,1,0:T(2,128)(2,1)}), bf16[584,1,1024]{2,1,0:T(2,128)(2,1)}) %all-gather.28.cloned.1.call-update) | async-done | bytes 1196048 | tf_op jit(solution)/shard_map/all_gather | solution.py:96
  89.3 26.4 %all-gather.20.cloned.1.call-done = bf16[3,1024,256]{2,1,0:T(8,128)(2,1)} async-done(((bf16[3,128,256]{2,1,0:T(8,128)(2,1)}), bf16[3,1024,256]{2,1,0:T(8,128)(2,1)}) %all-gather.20.cloned.1.call-update) | async-done | bytes 1572880 | tf_op jit(solution)/shard_map/all_gather | solution.py:68
  115.7 3.3 convolution_bitcast_fusion.6
  119.1 49.8 %all-gather.18.cloned.1.call-done = bf16[584,1,1024]{2,1,0:T(2,128)(2,1)} async-done(((bf16[146,1,1024]{2,1,0:T(2,128)(2,1)}), bf16[584,1,1024]{2,1,0:T(2,128)(2,1)}) %all-gather.18.cloned.1.call-update) | async-done | bytes 1196048 | tf_op jit(solution)/shard_map/all_gather | solution.py:96
  168.9 3.3 convolution_bitcast_fusion.7
  185.2 3.9 copy.127
  194.9 3.9 copy.133
  199.5 8.7 all-gather.2
  208.3 8.7 all-gather.3
  216.9 7.8 all-gather.4
  226.0 146.3 %all-reduce.30.cloned.1.call-done = (f32[584,1,1024]{2,1,0:T(1,128)}, f32[584,1,1024]{2,1,0:T(1,128)}) async-done(((f32[584,1,1024]{2,1,0:T(1,128)}, f32[584,1,1024]{2,1,0:T(1,128)}), (f32[584,1,1024]{2,1,0:T(1,128)}, f32[584,1,1024]{2,1,0:T(1,128)})) %all-reduce.30.cloned.1.call-update) | async-done | bytes 4784144
  372.3 4.0 fusion.112
  385.8 15.3 %all-gather.24.cloned.1.call-done = bf16[1024,1024]{1,0:T(8,128)(2,1)} async-done(((bf16[128,1024]{1,0:T(8,128)(2,1)}), bf16[1024,1024]{1,0:T(8,128)(2,1)}) %all-gather.24.cloned.1.call-update) | async-done | bytes 2097168 | tf_op jit(solution)/shard_map/all_gather | solution.py:70
  401.1 52.6 %all-gather.30.cloned.1.call-done = bf16[584,1,1024]{2,1,0:T(2,128)(2,1)} async-done(((bf16[146,1,1024]{2,1,0:T(2,128)(2,1)}), bf16[584,1,1024]{2,1,0:T(2,128)(2,1)}) %all-gather.30.cloned.1.call-update) | async-done | bytes 1196048 | tf_op jit(solution)/shard_map/all_gather | solution.py:137
  453.7 5.1 fusion.57
  458.8 47.0 %all-gather.22.cloned.1.call-done = bf16[584,1,1024]{2,1,0:T(2,128)(2,1)} async-done(((bf16[146,1,1024]{2,1,0:T(2,128)(2,1)}), bf16[584,1,1024]{2,1,0:T(2,128)(2,1)}) %all-gather.22.cloned.1.call-update) | async-done | bytes 1196048 | tf_op jit(solution)/shard_map/all_gather | solution.py:137
  505.7 16.0 %multiply_convert_fusion.3 = (bf16[584,1024]{1,0:T(8,128)(2,1)}, f32[584,1024]{1,0:T(8,128)}, bf16[584,1024]{1,0:T(8,128)(2,1)}, f32[584,1024]{1,0:T(8,128)}, f32[584,1024]{1,0:T(8,128)}) fusion(f32[1024]{0:T(1024)S(1)} %convert_element_type.338, f32[584,1024]{1,0:T(8,128)} %fusion.57, bf16[1024,1024]{1,0:T(8,128)(2,1)} %all-gather.24.cloned.1.call-done, ...), kind=kOutput, calls=%fused_computation.44 | convolution fusion | flops 1303674880 | bytes 15257600 | tf_op jit(solution)/shard_map/sid,df->sif/dot_general | solution.py:139
  521.8 13.0 all-gather.26.cloned.1.call-done
  534.8 4.6 fusion.26
  539.4 2.5 fusion.27
  541.9 48.2 %fusion.106 = (bf16[152,1024]{1,0:T(8,128)(2,1)S(1)}, bf16[152,1024]{1,0:T(8,128)(2,1)}) fusion(bf16[584,1,1024]{2,0,1:T(8,128)(2,1)} %fusion.27, bf16[584,1,1024]{2,0,1:T(8,128)(2,1)} %fusion.26), kind=kCustom, calls=%all-reduce-scatter.2 | all-reduce-scatter fusion | flops 1245185 | bytes 3015168
  590.9 3.4 collective-permute-start
  595.6 8.7 all-gather.5
  606.9 3.3 concatenate.10
  612.0 2.9 concatenate.11
  615.9 8.2 multiply_convert_fusion.5
  628.0 47.2 %all-gather.32.cloned.1.call-done = bf16[584,1,1024]{2,1,0:T(2,128)(2,1)} async-done(((bf16[146,1,1024]{2,1,0:T(2,128)(2,1)}), bf16[584,1,1024]{2,1,0:T(2,128)(2,1)}) %all-gather.32.cloned.1.call-update) | async-done | bytes 1196048 | tf_op jit(solution)/shard_map/all_gather | solution.py:157
  675.2 6.1 convert_reduce_fusion.1
  683.8 3.9 copy.135
  687.6 38.9 %all-gather.36.cloned.1.call-done = bf16[584,1,1024]{2,1,0:T(2,128)(2,1)} async-done(((bf16[146,1,1024]{2,1,0:T(2,128)(2,1)}), bf16[584,1,1024]{2,1,0:T(2,128)(2,1)}) %all-gather.36.cloned.1.call-update) | async-done | bytes 1196048 | tf_op jit(solution)/shard_map/all_gather | solution.py:157
  726.5 6.1 convert_reduce_fusion
  735.1 3.8 copy.144
  739.2 173.2 %all-reduce.28.cloned.1.call-done = (f32[584,1,1024]{2,1,0:T(1,128)}, f32[584,1,1024]{2,1,0:T(1,128)}) async-done(((f32[584,1,1024]{2,1,0:T(1,128)}, f32[584,1,1024]{2,1,0:T(1,128)}), (f32[584,1,1024]{2,1,0:T(1,128)}, f32[584,1,1024]{2,1,0:T(1,128)})) %all-reduce.28.cloned.1.call-update) | async-done | bytes 4784144
  912.3 5.0 multiply_reduce_fusion.3
  917.4 6.1 fusion.109
  929.7 46.1 %all-gather.34.cloned.1.call-done = bf16[584,1,1024]{2,1,0:T(2,128)(2,1)} async-done(((bf16[146,1,1024]{2,1,0:T(2,128)(2,1)}), bf16[584,1,1024]{2,1,0:T(2,128)(2,1)}) %all-gather.34.cloned.1.call-update) | async-done | bytes 1196048 | tf_op jit(solution)/shard_map/all_gather | solution.py:183
  975.7 2.9 convolution_convert_fusion.3
  979.8 4.4 multiply_reduce_fusion.1
  990.3 37.4 %all-gather.38.cloned.1.call-done = bf16[584,1,1024]{2,1,0:T(2,128)(2,1)} async-done(((bf16[146,1,1024]{2,1,0:T(2,128)(2,1)}), bf16[584,1,1024]{2,1,0:T(2,128)(2,1)}) %all-gather.38.cloned.1.call-update) | async-done | bytes 1196048 | tf_op jit(solution)/shard_map/all_gather | solution.py:183
  1030.2 3.9 convert_reduce_fusion.2
  1034.1 4.2 multiply_reduce_fusion
  1042.4 3.8 fusion.65
  1046.2 3.3 add_bitcast_fusion
  1049.6 2.5 convolution_bitcast_fusion.2
  1052.2 3.9 copy.143
  1057.2 3.8 copy.152
  1062.4 3.7 fusion.50
  1066.1 4.0 convolution_add_fusion
  1071.4 3.8 fusion.61
  1075.2 4.0 convolution_add_fusion.1
  1087.9 6.9 reduce-scatter.11.cloned.1.call-done
  1096.7 174.9 %all-reduce.26.cloned.1.call-done = (f32[584,1,1024]{2,1,0:T(1,128)}, f32[584,1,1024]{2,1,0:T(1,128)}) async-done(((f32[584,1,1024]{2,1,0:T(1,128)}, f32[584,1,1024]{2,1,0:T(1,128)}), (f32[584,1,1024]{2,1,0:T(1,128)}, f32[584,1,1024]{2,1,0:T(1,128)})) %all-reduce.26.cloned.1.call-update) | async-done | bytes 4784144
  1271.7 5.0 multiply_reduce_fusion.5
  1276.7 25.3 %all-reduce.16 = (f32[1024]{0:T(1024)S(1)}, f32[1024]{0:T(1024)S(1)}, f32[2,256]{1,0:T(2,128)}, f32[1024]{0:T(1024)S(1)}, f32[1024]{0:T(1024)S(1)}, /*index=5*/f...) all-reduce(f32[1024]{0:T(1024)S(1)} %add.380, ...), channel_id=10, replica_groups=mesh['dp'=8,'tensor'=4] {'dp'}, use_global_device_ids=true, to_apply=%region_33.34.clone | all-reduce | flops 7680 | bytes 61440
  1302.4 10.2 all-reduce.17
  1312.7 5.4 fusion.107
  1321.6 4.2 reduce-scatter.17.cloned.1.call-done
  1325.8 55.5 %reduce-scatter.15.cloned.1.call-done = f32[128,1024]{1,0:T(8,128)} async-done(((f32[1024,1024]{1,0:T(8,128)}), f32[128,1024]{1,0:T(8,128)}) %reduce-scatter.15.cloned.1.call-update) | async-done | bytes 524304 | tf_op jit(solution)/shard_map/reduce_scatter | solution.py:244
  1381.3 39.6 %reduce-scatter.13.cloned.1.call-done = f32[256,128]{1,0:T(8,128)} async-done(((f32[256,1024]{1,0:T(8,128)}), f32[256,128]{1,0:T(8,128)}) %reduce-scatter.13.cloned.1.call-update) | async-done | bytes 131088 | tf_op jit(solution)/shard_map/reduce_scatter | solution.py:243
  (290 shorter events, 86.9 us)
Async XLA Ops:
  7.2 82.1 %all-gather.28.cloned.1.call-start = ((), (), s32[]{:S(2)}) async-start(), calls=%async_computation.9 | async-start | bytes 2990080 | tf_op jit(solution)/shard_map/all_gather | solution.py:96
  20.7 17.1 %copy-start.38 = (f32[8,1,128]{2,1,0:T(1,128)}, f32[8,1,128]{2,1,0:T(1,128)S(1)}, u32[]{:S(2)}) copy-start(f32[8,1,128]{2,1,0:T(1,128)S(1)} %convert_element_type.404) | copy-start | bytes 12292
  34.5 84.5 %copy-start.48 = (f32[146]{0:T(256)}, f32[146]{0:T(256)S(1)}, u32[]{:S(2)}) copy-start(f32[146]{0:T(256)S(1)} %get-tuple-element.152) | copy-start | bytes 1756
  34.5 4.8 copy-start.52
  34.5 5.0 copy-start.45
  34.6 5.0 copy-start.40
  37.8 77.9 %all-gather.20.cloned.1.call-start = ((), (), s32[]{:S(2)}) async-start(), calls=%async_computation.5 | async-start | bytes 1769472 | tf_op jit(solution)/shard_map/all_gather | solution.py:68
  38.5 130.4 %all-gather.18.cloned.1.call-start = ((), (), s32[]{:S(2)}) async-start(), calls=%async_computation.4 | async-start | bytes 2990080 | tf_op jit(solution)/shard_map/all_gather | solution.py:96
  39.3 333.0 %all-reduce.30.cloned.1.call-start = ((), (), s32[]{:S(2)}) async-start(), calls=%async_computation.21 | async-start | bytes 9568256
  49.2 145.2 %copy-start.15 = (bf16[256,1024]{1,0:T(8,128)(2,1)}, bf16[256,1024]{1,0:T(8,128)(2,1)S(1)}, u32[]{:S(2)}) copy-start(bf16[256,1024]{1,0:T(8,128)(2,1)S(1)} %all_gather.68) | copy-start | bytes 1572868
  174.5 17.1 %copy-start.19 = (f32[1,584,1,256]{1,3,2,0:T(8,128)}, f32[1,584,1,256]{1,3,2,0:T(8,128)S(1)}, u32[]{:S(2)}) copy-start(f32[1,584,1,256]{1,3,2,0:T(8,128)S(1)} %copy.129) | copy-start | bytes 1794052
  175.9 5.0 copy-start.17
  184.7 4.4 copy-start.25
  194.4 4.5 copy-start.27
  198.8 9.4 copy-start.54
  198.8 18.1 %copy-start.55 = (bf16[128]{0:T(256)(128)(2,1)S(1)}, bf16[128]{0:T(256)(128)(2,1)}, u32[]{:S(2)}) copy-start(bf16[128]{0:T(256)(128)(2,1)} %param.27) | copy-start | bytes 772
  198.8 25.9 %copy-start.51 = (u32[32]{0:T(128)S(1)}, u32[32]{0:T(128)}, u32[]{:S(2)}) copy-start(u32[32]{0:T(128)} %constant.109) | copy-start | bytes 388
  198.8 173.4 %copy-start.2 = (bf16[146,2,1024]{2,1,0:T(2,128)(2,1)S(1)}, bf16[146,2,1024]{2,1,0:T(2,128)(2,1)}, u32[]{:S(2)}) copy-start(bf16[146,2,1024]{2,1,0:T(2,128)(2,1)} %param.16) | copy-start | bytes 1794052
  198.9 202.2 %all-gather.24.cloned.1.call-start = ((), (), s32[]{:S(2)}) async-start(), calls=%async_computation.7 | async-start | bytes 2359296 | tf_op jit(solution)/shard_map/all_gather | solution.py:70
  199.5 254.2 %all-gather.30.cloned.1.call-start = ((), (), s32[]{:S(2)}) async-start(), calls=%async_computation.10 | async-start | bytes 2990080 | tf_op jit(solution)/shard_map/all_gather | solution.py:137
  376.3 6.4 copy-start.13
  376.3 6.4 copy-start.14
  378.3 7.4 copy-start.50
  382.7 123.1 %all-gather.22.cloned.1.call-start = ((), (), s32[]{:S(2)}) async-start(), calls=%async_computation.6 | async-start | bytes 2990080 | tf_op jit(solution)/shard_map/all_gather | solution.py:137
  383.4 151.4 %all-gather.26.cloned.1.call-start = ((), (), s32[]{:S(2)}) async-start(), calls=%async_computation.8 | async-start | bytes 2359296 | tf_op jit(solution)/shard_map/all_gather | solution.py:71
  384.2 291.0 %all-gather.32.cloned.1.call-start = ((), (), s32[]{:S(2)}) async-start(), calls=%async_computation.11 | async-start | bytes 2990080 | tf_op jit(solution)/shard_map/all_gather | solution.py:157
  534.8 4.6 copy-start.30
  534.8 4.6 copy-start.59
  541.9 53.6 %copy-start.56 = (bf16[128]{0:T(256)(128)(2,1)S(1)}, bf16[128]{0:T(256)(128)(2,1)}, u32[]{:S(2)}) copy-start(bf16[128]{0:T(256)(128)(2,1)} %param.31) | copy-start | bytes 772
  590.9 16.0 %collective-permute-start = (bf16[18,1024]{1,0:T(8,128)(2,1)S(1)}, bf16[18,1024]{1,0:T(8,128)(2,1)S(1)}, u32[]{:S(2)}, u32[]{:S(2)}) collective-permute-start(bf16[18,1024]{1,0:T(8,128)(2,1)S(1)} %slice.94), channel_id=1, source_target_pairs={{0,1},{1,2},{2,3},{4,5},{5,6},{6,7},{8,9},{9,10},{10,11},{12,13},{... | collective-permute-start | bytes 110600
  605.0 7.0 collective-permute-start.1
  624.1 57.2 %copy-start.9 = (f32[146,1,1024]{2,1,0:T(1,128)}, f32[146,1,1024]{2,1,0:T(1,128)S(1)}, u32[]{:S(2)}) copy-start(f32[146,1,1024]{2,1,0:T(1,128)S(1)} %get-tuple-element.173) | copy-start | bytes 1794052
  626.2 100.4 %all-gather.36.cloned.1.call-start = ((), (), s32[]{:S(2)}) async-start(), calls=%async_computation.13 | async-start | bytes 2990080 | tf_op jit(solution)/shard_map/all_gather | solution.py:157
  627.5 284.9 %all-reduce.28.cloned.1.call-start = ((), (), s32[]{:S(2)}) async-start(), calls=%async_computation.20 | async-start | bytes 9568256
  675.2 7.2 copy-start.57
  726.5 7.1 copy-start.58
  738.9 236.8 %all-gather.34.cloned.1.call-start = ((), (), s32[]{:S(2)}) async-start(), calls=%async_computation.12 | async-start | bytes 2990080 | tf_op jit(solution)/shard_map/all_gather | solution.py:183
  917.3 6.1 copy-start.12
  925.5 50.2 %copy-start.16 = (bf16[256,1024]{1,0:T(8,128)(2,1)S(1)}, bf16[256,1024]{1,0:T(8,128)(2,1)}, u32[]{:S(2)}) copy-start(bf16[256,1024]{1,0:T(8,128)(2,1)} %copy-done.15) | copy-start | bytes 1572868
  925.5 102.2 %all-gather.38.cloned.1.call-start = ((), (), s32[]{:S(2)}) async-start(), calls=%async_computation.14 | async-start | bytes 2990080 | tf_op jit(solution)/shard_map/all_gather | solution.py:183
  929.6 165.2 %reduce-scatter.11.cloned.1.call-start = ((), (), s32[]{:S(2)}) async-start(), calls=%async_computation.15 | async-start | bytes 3538944 | tf_op jit(solution)/shard_map/reduce_scatter | solution.py:242
  979.8 4.5 slice-start.2
  979.8 5.0 slice-start.3
  1030.1 4.0 copy-start.20
  1030.1 8.2 slice-start
  1034.1 4.2 slice-start.1
  1042.4 3.8 copy-start.34
  1049.6 222.0 %all-reduce.26.cloned.1.call-start = ((), (), s32[]{:S(2)}) async-start(), calls=%async_computation.19 | async-start | bytes 9568256
  1052.2 3.9 copy-start.60
  1061.1 5.0 copy-start.31
  1061.1 264.7 %reduce-scatter.17.cloned.1.call-start = ((), (), s32[]{:S(2)}) async-start(), calls=%async_computation.18 | async-start | bytes 4718592 | tf_op jit(solution)/shard_map/reduce_scatter | solution.py:245
  1070.1 5.1 copy-start.33
  1070.1 311.2 %reduce-scatter.15.cloned.1.call-start = ((), (), s32[]{:S(2)}) async-start(), calls=%async_computation.17 | async-start | bytes 4718592 | tf_op jit(solution)/shard_map/reduce_scatter | solution.py:244
  1079.3 4.4 copy-start.26
  1079.3 6.9 copy-start.28
  1079.3 341.6 %reduce-scatter.13.cloned.1.call-start = ((), (), s32[]{:S(2)}) async-start(), calls=%async_computation.16 | async-start | bytes 1179648 | tf_op jit(solution)/shard_map/reduce_scatter | solution.py:243
  1086.2 185.4 %copy-start.4 = (f32[146,1,1024]{2,1,0:T(1,128)S(1)}, f32[146,1,1024]{2,1,0:T(1,128)}, u32[]{:S(2)}) copy-start(f32[146,1,1024]{2,1,0:T(1,128)} %copy-done.3) | copy-start | bytes 1794052
  1086.2 185.4 %copy-start.6 = (f32[146,1,1024]{2,1,0:T(1,128)S(1)}, f32[146,1,1024]{2,1,0:T(1,128)}, u32[]{:S(2)}) copy-start(f32[146,1,1024]{2,1,0:T(1,128)} %copy-done.5) | copy-start | bytes 1794052
  1086.2 185.4 %copy-start.39 = (f32[8,1,128]{2,1,0:T(1,128)S(1)}, f32[8,1,128]{2,1,0:T(1,128)}, u32[]{:S(2)}) copy-start(f32[8,1,128]{2,1,0:T(1,128)} %copy-done.38) | copy-start | bytes 12292
  1086.2 185.4 %copy-start.42 = (f32[146]{0:T(256)S(1)}, f32[146]{0:T(256)}, u32[]{:S(2)}) copy-start(f32[146]{0:T(256)} %copy-done.41) | copy-start | bytes 1756
  1086.2 185.4 %copy-start.44 = (f32[146]{0:T(256)S(1)}, f32[146]{0:T(256)}, u32[]{:S(2)}) copy-start(f32[146]{0:T(256)} %copy-done.43) | copy-start | bytes 1756
  1087.9 188.8 %copy-start.49 = (f32[146]{0:T(256)S(1)}, f32[146]{0:T(256)}, u32[]{:S(2)}) copy-start(f32[146]{0:T(256)} %copy-done.48) | copy-start | bytes 1756
  1087.9 188.8 %copy-start.47 = (f32[146]{0:T(256)S(1)}, f32[146]{0:T(256)}, u32[]{:S(2)}) copy-start(f32[146]{0:T(256)} %copy-done.46) | copy-start | bytes 1756
  1312.7 6.1 copy-start.8
  (25 other events, 45.0 us)
Sparse Core Ops, SparseCore 0:
  37.9 51.3 all-gather.27
  91.2 24.4 all-gather.19
  117.8 51.0 all-gather.17
  199.0 173.2 all-reduce.29
  374.2 26.8 all-gather.23
  402.6 51.0 all-gather.29
  455.9 49.8 all-gather.21
  507.8 26.9 all-gather.25
  626.3 48.8 all-gather.31
  676.6 49.8 all-gather.35
  739.1 173.2 all-reduce.27
  925.7 50.0 all-gather.33
  977.8 49.8 all-gather.37
  1049.7 45.0 reduce-scatter.10
  1097.2 174.4 all-reduce.25
  1275.4 50.3 reduce-scatter.16
  1329.9 51.3 reduce-scatter.14
  1384.9 35.9 reduce-scatter.12
where the time goes:
time: 1430 us
  waiting for transfers between devices  1020 us (71%)
  blocking collectives  146 us (10%)
  matrix products  110 us (8%)
  other arithmetic  69.8 us (5%)
  local copies, waits for them, and re-layouts  58.6 us (4%)
  between operations  18.3 us (1%)
    unnamed x23, waiting for transfers between devices  498 us
    all_gather x2, waiting for transfers between devices, per_device(): normed2_all = lax.all_gather(normed2, 'tensor', axis=0, tiled=True)  99.5 us
    all_gather x2, waiting for transfers between devices, per_device(): normed_all = lax.all_gather(normed, 'tensor', axis=0, tiled=True)  89.8 us
    all_gather x2, waiting for transfers between devices, per_device(): mlp_grad_all = lax.all_gather(mlp_grad, 'tensor', axis=0, tiled=True)  86.1 us
    all_gather x2, waiting for transfers between devices, per_device(): branch_all = lax.all_gather(branch_grad, 'tensor', axis=0, tiled=True)  83.5 us
    unnamed x2, blocking collectives  73.4 us
    reduce_scatter x1, waiting for transfers between devices, per_device(): lax.psum_scatter(acc_up, 'dp', scatter_dimension=0, tiled=True)  55.5 us
    reduce_scatter x1, waiting for transfers between devices, per_device(): lax.psum_scatter(acc_proj, 'dp', scatter_dimension=1, tiled=True)  39.6 us
  transfers between devices with their start and end apart: 20, of which 18 were waited for; matrix products, arithmetic and copies ran while one was open for 9% of the time, Pallas kernels for 0%

commit v1 on v0

--- a/solution.py
+++ b/solution.py
@@ -9,6 +9,35 @@
 MB = 2
 EPS = 1e-06
 NEG = -1000000000.0
+
+
+def feed_node(message, along_dim):
+    out_arr = lax.axis_size("tensor")
+    d_next = lax.axis_index("tensor")
+    frame_out, part_now, a_now = (out_arr, d_next, message.shape[along_dim])
+    line_up = []
+    for j0, ix in enumerate(message.shape):
+        line_up.append(ix * frame_out if j0 == along_dim else ix)
+    even = jnp.zeros(line_up, message.dtype)
+    a_next = lax.dynamic_update_slice_in_dim(even, message, part_now * a_now, axis=along_dim)
+    reply = low = message
+    for dev_j in [*range(1, frame_out // 2 + 1)]:
+        buffers = []
+        for j0 in [*range(frame_out)]:
+            buffers.append((j0, (j0 + 1) % frame_out))
+        reply = lax.ppermute(reply, axis_name="tensor", perm=buffers)
+        a_next = lax.dynamic_update_slice_in_dim(
+            a_next, reply, (part_now - dev_j) % frame_out * a_now, axis=along_dim
+        )
+        if 2 * dev_j < frame_out:
+            windows = []
+            for j0 in [*range(frame_out)]:
+                windows.append((j0, (j0 - 1) % frame_out))
+            low = lax.ppermute(low, axis_name="tensor", perm=windows)
+            a_next = lax.dynamic_update_slice_in_dim(
+                a_next, low, (part_now + dev_j) % frame_out * a_now, axis=along_dim
+            )
+    return a_next
 
 
 def layer_norm(values, gain, shift):
@@ -180,7 +209,7 @@
         resid_grad = outer + resid_part
         branch_grad = resid_grad.astype(bf16)
         acc_vectors[2] = acc_vectors[2] + jnp.sum(branch_grad.astype(f32), axis=(0, 1))
-        branch_all = lax.all_gather(branch_grad, "tensor", axis=0, tiled=True)
+        branch_all = feed_node(branch_grad, 0)
         acc_proj = acc_proj + jnp.einsum(
             "sie,sid->ed", attended, branch_all, preferred_element_type=f32
         )

time: 1430 us -> 1340 us (0.937)
  waiting for transfers between devices: 1020 us -> 857 us
  other arithmetic: 69.8 us -> 24.3 us
  local copies, waits for them, and re-layouts: 58.6 us -> 104 us
  blocking collectives: 146 us -> 186 us
  starting transfers between devices: 7.04 us -> 36.5 us
    unnamed x23 -> x21, waiting for transfers between devices: 498 us -> 407 us
    all_gather x2 -> x0, waiting for transfers between devices: 83.5 us -> none  [per_device(): branch_all = lax.all_gather(branch_grad, 'tensor', axis=0, tiled=True)]
    reduce_scatter x1, waiting for transfers between devices: 4.22 us -> 55.5 us  [per_device(): lax.psum_scatter(acc_down, 'dp', scatter_dimension=1, tiled=True)]
    reduce_scatter x1, waiting for transfers between devices: 55.5 us -> 9.88 us  [per_device(): lax.psum_scatter(acc_up, 'dp', scatter_dimension=0, tiled=True)]
    unnamed x2, blocking collectives: 73.4 us -> 113 us
    dynamic_update_slice x0 -> x8, local copies, waits for them, and re-layouts: none -> 21.6 us  [the longest x4 11.3 us: feed_node(): lax.dynamic_update_slice_in_dim(a_next, reply, (part_now - dev_j) % frame...]
    reduce_sum x4, other arithmetic: 18.6 us -> 2.29 us  [layer_norm(): center = values - jnp.mean(values, axis=-1, keepdims=True)]
    ppermute x0 -> x6, starting transfers between devices: none -> 16.2 us  [the longest x4 8.53 us: feed_node(): reply = lax.ppermute(reply, axis_name='tensor', perm=buffers)]
  transfers between devices with their start and end apart: 20 -> 24, of which waited for: 18 -> 18; matrix products, arithmetic and copies ran while one was open for 9% -> 18% of each run, Pallas kernels for 0% -> 0%
where the time goes in v1:
time: 1340 us
  waiting for transfers between devices  857 us (64%)
  blocking collectives  186 us (14%)
  matrix products  111 us (8%)
  local copies, waits for them, and re-layouts  104 us (8%)
  starting transfers between devices  36.5 us (3%)
  other arithmetic  24.3 us (2%)
  between operations  18.3 us (1%)
    unnamed x21, waiting for transfers between devices  407 us
    unnamed x2, blocking collectives  113 us
    all_gather x2, waiting for transfers between devices, per_device(): normed2_all = lax.all_gather(normed2, 'tensor', axis=0, tiled=True)  100 us
    all_gather x2, waiting for transfers between devices, per_device(): normed_all = lax.all_gather(normed, 'tensor', axis=0, tiled=True)  88.8 us
    all_gather x2, waiting for transfers between devices, per_device(): mlp_grad_all = lax.all_gather(mlp_grad, 'tensor', axis=0, tiled=True)  74.9 us
    reduce_scatter x1, waiting for transfers between devices, per_device(): lax.psum_scatter(acc_down, 'dp', scatter_dimension=1, tiled=True)  55.5 us
    reduce_scatter x1, waiting for transfers between devices, per_device(): lax.psum_scatter(acc_proj, 'dp', scatter_dimension=1, tiled=True)  39.6 us
    all_gather x1, waiting for transfers between devices, per_device(): lax.all_gather(down_weight, 'dp', axis=1, tiled=True)  29.1 us
  transfers between devices with their start and end apart: 24, of which 18 were waited for; matrix products, arithmetic and copies ran while one was open for 18% of the time, Pallas kernels for 0%

profile of v1, /device:TPU:0, one launch (start us, length us, event | category | flops | bytes accessed | tf_op | source)
XLA Modules:
  0.0 1335.9 jit_solution(11904981683167045099)
XLA Ops:
  11.6 10.2 all-gather
  21.8 8.7 all-gather.1
  34.5 9.2 all_gather.62
  43.7 39.9 %all-gather.16.cloned.1.call-done = bf16[584,1,1024]{2,1,0:T(2,128)(2,1)} async-done(((bf16[146,1,1024]{2,1,0:T(2,128)(2,1)}), bf16[584,1,1024]{2,1,0:T(2,128)(2,1)}) %all-gather.16.cloned.1.call-update) | async-done | bytes 1196048 | tf_op jit(solution)/shard_map/all_gather | solution.py:125
  83.6 26.4 %all-gather.18.cloned.1.call-done = bf16[3,1024,256]{2,1,0:T(8,128)(2,1)} async-done(((bf16[3,128,256]{2,1,0:T(8,128)(2,1)}), bf16[3,1024,256]{2,1,0:T(8,128)(2,1)}) %all-gather.18.cloned.1.call-update) | async-done | bytes 1572880 | tf_op jit(solution)/shard_map/all_gather | solution.py:97
  110.0 3.3 convolution_bitcast_fusion.7
  114.2 49.0 %all-gather.26.cloned.1.call-done = bf16[584,1,1024]{2,1,0:T(2,128)(2,1)} async-done(((bf16[146,1,1024]{2,1,0:T(2,128)(2,1)}), bf16[584,1,1024]{2,1,0:T(2,128)(2,1)}) %all-gather.26.cloned.1.call-update) | async-done | bytes 1196048 | tf_op jit(solution)/shard_map/all_gather | solution.py:125
  163.2 3.3 convolution_bitcast_fusion.6
  176.0 3.9 copy.129
  188.7 3.9 copy.138
  193.4 8.7 all-gather.2
  202.1 8.7 all-gather.3
  210.8 7.8 all-gather.4
  219.8 146.3 %all-reduce.30.cloned.1.call-done = (f32[584,1,1024]{2,1,0:T(1,128)}, f32[584,1,1024]{2,1,0:T(1,128)}) async-done(((f32[584,1,1024]{2,1,0:T(1,128)}, f32[584,1,1024]{2,1,0:T(1,128)}), (f32[584,1,1024]{2,1,0:T(1,128)}, f32[584,1,1024]{2,1,0:T(1,128)})) %all-reduce.30.cloned.1.call-update) | async-done | bytes 4784144
  381.6 13.3 all-gather.22.cloned.1.call-done
  394.9 53.1 %all-gather.28.cloned.1.call-done = bf16[584,1,1024]{2,1,0:T(2,128)(2,1)} async-done(((bf16[146,1,1024]{2,1,0:T(2,128)(2,1)}), bf16[584,1,1024]{2,1,0:T(2,128)(2,1)}) %all-gather.28.cloned.1.call-update) | async-done | bytes 1196048 | tf_op jit(solution)/shard_map/all_gather | solution.py:166
  448.1 5.2 fusion.52
  453.2 46.9 %all-gather.20.cloned.1.call-done = bf16[584,1,1024]{2,1,0:T(2,128)(2,1)} async-done(((bf16[146,1,1024]{2,1,0:T(2,128)(2,1)}), bf16[584,1,1024]{2,1,0:T(2,128)(2,1)}) %all-gather.20.cloned.1.call-update) | async-done | bytes 1196048 | tf_op jit(solution)/shard_map/all_gather | solution.py:166
  500.1 16.2 %multiply_convert_fusion.3 = (bf16[584,1024]{1,0:T(8,128)(2,1)}, f32[584,1024]{1,0:T(8,128)}, bf16[584,1024]{1,0:T(8,128)(2,1)}, f32[584,1024]{1,0:T(8,128)}, f32[584,1024]{1,0:T(8,128)}) fusion(f32[1024]{0:T(1024)S(1)} %convert_element_type.338, f32[584,1024]{1,0:T(8,128)} %fusion.52, bf16[1024,1024]{1,0:T(8,128)(2,1)} %all-gather.22.cloned.1.call-done, ...), kind=kOutput, calls=%fused_computation.44 | convolution fusion | flops 1303674880 | bytes 15257600 | tf_op jit(solution)/shard_map/sid,df->sif/dot_general | solution.py:168
  516.3 35.3 %all-gather.30.cloned.1.call-done = bf16[584,1,1024]{2,1,0:T(2,128)(2,1)} async-done(((bf16[146,1,1024]{2,1,0:T(2,128)(2,1)}), bf16[584,1,1024]{2,1,0:T(2,128)(2,1)}) %all-gather.30.cloned.1.call-update) | async-done | bytes 1196048 | tf_op jit(solution)/shard_map/all_gather | solution.py:186
  551.7 29.1 %all-gather.24.cloned.1.call-done = bf16[1024,1024]{1,0:T(8,128)(2,1)} async-done(((bf16[1024,128]{1,0:T(8,128)(2,1)}), bf16[1024,1024]{1,0:T(8,128)(2,1)}) %all-gather.24.cloned.1.call-update) | async-done | bytes 2097168 | tf_op jit(solution)/shard_map/all_gather | solution.py:100
  580.7 6.7 convert_reduce_fusion.1
  589.9 3.8 copy.143
  593.7 39.5 %all-gather.32.cloned.1.call-done = bf16[584,1,1024]{2,1,0:T(2,128)(2,1)} async-done(((bf16[146,1,1024]{2,1,0:T(2,128)(2,1)}), bf16[584,1,1024]{2,1,0:T(2,128)(2,1)}) %all-gather.32.cloned.1.call-update) | async-done | bytes 1196048 | tf_op jit(solution)/shard_map/all_gather | solution.py:186
  633.3 6.7 convert_reduce_fusion
  642.4 3.9 copy.156
  646.6 4.6 fusion.26
  653.6 88.4 %fusion.117 = (bf16[152,1024]{1,0:T(8,128)(2,1)S(1)}, bf16[152,1024]{1,0:T(8,128)(2,1)}) fusion(bf16[584,1,1024]{2,0,1:T(8,128)(2,1)} %fusion.27, bf16[584,1,1024]{2,0,1:T(8,128)(2,1)} %fusion.26), kind=kCustom, calls=%all-reduce-scatter.2 | all-reduce-scatter fusion | flops 1245185 | bytes 3015168
  743.5 14.4 %collective-permute-start.6 = (bf16[18,1024]{1,0:T(8,128)(2,1)}, bf16[18,1024]{1,0:T(8,128)(2,1)S(1)}, u32[]{:S(2)}, u32[]{:S(2)}) collective-permute-start(bf16[18,1024]{1,0:T(8,128)(2,1)} %slice.94), channel_id=1, source_target_pairs={{0,1},{1,2},{2,3},{4,5},{5,6},{6,7},{8,9},{9,10},{10,11},{12,13},{... | collective-permute-start | bytes 110600
  757.9 4.7 collective-permute-start.7
  762.6 8.8 all-gather.5
  772.2 3.3 concatenate.10
  775.4 2.9 concatenate.11
  778.3 83.0 %all-reduce.28.cloned.1.call-done = (f32[584,1,1024]{2,1,0:T(1,128)}, f32[584,1,1024]{2,1,0:T(1,128)}) async-done(((f32[584,1,1024]{2,1,0:T(1,128)}, f32[584,1,1024]{2,1,0:T(1,128)}), (f32[584,1,1024]{2,1,0:T(1,128)}, f32[584,1,1024]{2,1,0:T(1,128)})) %all-reduce.28.cloned.1.call-update) | async-done | bytes 4784144
  861.3 3.2 fusion.120
  868.9 3.8 collective-permute-start.1
  874.2 3.8 collective-permute-start.4
  878.0 3.0 collective-permute-done
  881.0 4.1 collective-permute-start.2
  888.3 2.8 dynamic_update_slice.36
  891.2 2.7 dynamic_update_slice.33
  898.0 2.9 dynamic_update_slice.34
  900.9 2.8 dynamic_update_slice.38
  903.7 4.4 collective-permute-start.5
  908.1 2.8 dynamic_update_slice.35
  915.3 4.5 multiply_reduce_fusion.1
  927.2 3.2 dynamic_update_slice.39
  932.9 4.4 multiply_reduce_fusion
  949.8 3.6 fusion.60
  953.4 3.3 add_bitcast_fusion
  956.9 2.8 convolution_bitcast_fusion.2
  959.8 3.9 copy.152
  964.8 3.9 copy.165
  968.8 4.2 fusion.56
  973.1 4.0 convolution_add_fusion.1
  977.4 4.5 fusion.45
  982.0 4.1 convolution_add_fusion
  993.8 9.0 reduce-scatter.11.cloned.1.call-done
  1004.7 175.1 %all-reduce.26.cloned.1.call-done = (f32[584,1,1024]{2,1,0:T(1,128)}, f32[584,1,1024]{2,1,0:T(1,128)}) async-done(((f32[584,1,1024]{2,1,0:T(1,128)}, f32[584,1,1024]{2,1,0:T(1,128)}), (f32[584,1,1024]{2,1,0:T(1,128)}, f32[584,1,1024]{2,1,0:T(1,128)})) %all-reduce.26.cloned.1.call-update) | async-done | bytes 4784144
  1185.9 24.8 %all-reduce.16 = (f32[1024]{0:T(1024)S(1)}, f32[1024]{0:T(1024)S(1)}, f32[2,256]{1,0:T(2,128)}, f32[1024]{0:T(1024)S(1)}, f32[1024]{0:T(1024)S(1)}, /*index=5*/f...) all-reduce(f32[1024]{0:T(1024)S(1)} %add.420, ...), channel_id=10, replica_groups=mesh['dp'=8,'tensor'=4] {'dp'}, use_global_device_ids=true, to_apply=%region_33.34.clone | all-reduce | flops 7680 | bytes 61440
  1213.9 10.2 all-reduce.17
  1224.1 9.9 reduce-scatter.15.cloned.1.call-done
  1234.0 55.5 %reduce-scatter.17.cloned.1.call-done = f32[1024,128]{1,0:T(8,128)} async-done(((f32[1024,1024]{1,0:T(8,128)}), f32[1024,128]{1,0:T(8,128)}) %reduce-scatter.17.cloned.1.call-update) | async-done | bytes 524304 | tf_op jit(solution)/shard_map/reduce_scatter | solution.py:274
  1289.5 39.6 %reduce-scatter.13.cloned.1.call-done = f32[256,128]{1,0:T(8,128)} async-done(((f32[256,1024]{1,0:T(8,128)}), f32[256,128]{1,0:T(8,128)}) %reduce-scatter.13.cloned.1.call-update) | async-done | bytes 131088 | tf_op jit(solution)/shard_map/reduce_scatter | solution.py:272
  (367 shorter events, 111.5 us)
Async XLA Ops:
  7.2 14.6 %copy-start.78 = (bf16[128]{0:T(256)(128)(2,1)S(1)}, bf16[128]{0:T(256)(128)(2,1)}, u32[]{:S(2)}) copy-start(bf16[128]{0:T(256)(128)(2,1)} %param.21) | copy-start | bytes 772
  7.2 76.4 %all-gather.16.cloned.1.call-start = ((), (), s32[]{:S(2)}) async-start(), calls=%async_computation.4 | async-start | bytes 2990080 | tf_op jit(solution)/shard_map/all_gather | solution.py:125
  9.9 359.2 %copy-start.2 = (bf16[146,1,1024]{2,0,1:T(8,128)(2,1)}, bf16[146,1,1024]{2,0,1:T(8,128)(2,1)S(1)}, u32[]{:S(2)}) copy-start(bf16[146,1,1024]{2,0,1:T(8,128)(2,1)S(1)} %get-tuple-element.138) | copy-start | bytes 897028
  9.9 24.3 %copy-start.47 = (f32[146]{0:T(256)}, f32[146]{0:T(256)S(1)}, u32[]{:S(2)}) copy-start(f32[146]{0:T(256)S(1)} %broadcast_multiply_fusion.1) | copy-start | bytes 1756
  10.1 24.0 %copy-start.51 = (f32[146]{0:T(256)}, f32[146]{0:T(256)S(1)}, u32[]{:S(2)}) copy-start(f32[146]{0:T(256)S(1)} %fusion.109) | copy-start | bytes 1756
  10.7 358.4 %copy-start.4 = (bf16[146,1,1024]{2,0,1:T(8,128)(2,1)}, bf16[146,1,1024]{2,0,1:T(8,128)(2,1)S(1)}, u32[]{:S(2)}) copy-start(bf16[146,1,1024]{2,0,1:T(8,128)(2,1)S(1)} %get-tuple-element.136) | copy-start | bytes 897028
  10.7 23.5 %copy-start.49 = (f32[146]{0:T(256)}, f32[146]{0:T(256)S(1)}, u32[]{:S(2)}) copy-start(f32[146]{0:T(256)S(1)} %broadcast_multiply_fusion.3) | copy-start | bytes 1756
  10.7 23.6 %copy-start.76 = (bf16[2,256]{1,0:T(2,128)(2,1)S(1)}, bf16[2,256]{1,0:T(2,128)(2,1)}, u32[]{:S(2)}) copy-start(bf16[2,256]{1,0:T(2,128)(2,1)} %param.23) | copy-start | bytes 3076
  10.7 23.8 %copy-start.61 = (s32[2,584]{1,0:T(2,128)S(1)}, s32[2,584]{1,0:T(2,128)}, u32[]{:S(2)}) copy-start(s32[2,584]{1,0:T(2,128)} %param.18) | copy-start | bytes 14020
  10.7 23.8 %copy-start.46 = (bf16[256,128]{1,0:T(8,128)(2,1)S(1)}, bf16[256,128]{1,0:T(8,128)(2,1)}, u32[]{:S(2)}) copy-start(bf16[256,128]{1,0:T(8,128)(2,1)} %param.24) | copy-start | bytes 196612
  11.6 32.2 %copy-start.53 = (f32[146]{0:T(256)}, f32[146]{0:T(256)S(1)}, u32[]{:S(2)}) copy-start(f32[146]{0:T(256)S(1)} %fusion.107) | copy-start | bytes 1756
  21.8 22.0 %copy-start.44 = (f32[8,1,128]{2,1,0:T(1,128)}, f32[8,1,128]{2,1,0:T(1,128)S(1)}, u32[]{:S(2)}) copy-start(f32[8,1,128]{2,1,0:T(1,128)S(1)} %convert_element_type.404) | copy-start | bytes 12292
  32.1 77.9 %all-gather.18.cloned.1.call-start = ((), (), s32[]{:S(2)}) async-start(), calls=%async_computation.5 | async-start | bytes 1769472 | tf_op jit(solution)/shard_map/all_gather | solution.py:97
  32.9 130.4 %all-gather.26.cloned.1.call-start = ((), (), s32[]{:S(2)}) async-start(), calls=%async_computation.9 | async-start | bytes 2990080 | tf_op jit(solution)/shard_map/all_gather | solution.py:125
  34.2 331.9 %all-reduce.30.cloned.1.call-start = ((), (), s32[]{:S(2)}) async-start(), calls=%async_computation.19 | async-start | bytes 9568256
  192.7 9.4 copy-start.80
  192.7 18.1 %copy-start.81 = (bf16[128]{0:T(256)(128)(2,1)S(1)}, bf16[128]{0:T(256)(128)(2,1)}, u32[]{:S(2)}) copy-start(bf16[128]{0:T(256)(128)(2,1)} %param.27) | copy-start | bytes 772
  192.7 25.9 %copy-start.75 = (u32[32]{0:T(128)S(1)}, u32[32]{0:T(128)}, u32[]{:S(2)}) copy-start(u32[32]{0:T(128)} %constant.152) | copy-start | bytes 388
  192.7 202.2 %all-gather.22.cloned.1.call-start = ((), (), s32[]{:S(2)}) async-start(), calls=%async_computation.7 | async-start | bytes 2359296 | tf_op jit(solution)/shard_map/all_gather | solution.py:99
  193.3 254.8 %all-gather.28.cloned.1.call-start = ((), (), s32[]{:S(2)}) async-start(), calls=%async_computation.10 | async-start | bytes 2990080 | tf_op jit(solution)/shard_map/all_gather | solution.py:166
  371.5 128.7 %all-gather.20.cloned.1.call-start = ((), (), s32[]{:S(2)}) async-start(), calls=%async_computation.6 | async-start | bytes 2990080 | tf_op jit(solution)/shard_map/all_gather | solution.py:166
  372.8 178.8 %all-gather.30.cloned.1.call-start = ((), (), s32[]{:S(2)}) async-start(), calls=%async_computation.11 | async-start | bytes 2990080 | tf_op jit(solution)/shard_map/all_gather | solution.py:186
  379.3 201.4 %all-gather.24.cloned.1.call-start = ((), (), s32[]{:S(2)}) async-start(), calls=%async_computation.8 | async-start | bytes 2359296 | tf_op jit(solution)/shard_map/all_gather | solution.py:100
  380.1 253.2 %all-gather.32.cloned.1.call-start = ((), (), s32[]{:S(2)}) async-start(), calls=%async_computation.12 | async-start | bytes 2990080 | tf_op jit(solution)/shard_map/all_gather | solution.py:186
  381.6 479.7 %all-reduce.28.cloned.1.call-start = ((), (), s32[]{:S(2)}) async-start(), calls=%async_computation.18 | async-start | bytes 9568256
  580.7 7.7 copy-start.83
  633.3 7.7 copy-start.84
  646.3 356.5 %reduce-scatter.11.cloned.1.call-start = ((), (), s32[]{:S(2)}) async-start(), calls=%async_computation.13 | async-start | bytes 3538944 | tf_op jit(solution)/shard_map/reduce_scatter | solution.py:271
  646.6 4.6 copy-start.37
  646.6 4.6 copy-start.85
  653.6 109.0 %copy-start.82 = (bf16[128]{0:T(256)(128)(2,1)S(1)}, bf16[128]{0:T(256)(128)(2,1)}, u32[]{:S(2)}) copy-start(bf16[128]{0:T(256)(128)(2,1)} %param.31) | copy-start | bytes 772
  743.5 28.7 %collective-permute-start.6 = (bf16[18,1024]{1,0:T(8,128)(2,1)}, bf16[18,1024]{1,0:T(8,128)(2,1)S(1)}, u32[]{:S(2)}, u32[]{:S(2)}) collective-permute-start(bf16[18,1024]{1,0:T(8,128)(2,1)} %slice.94), channel_id=1, source_target_pairs={{0,1},{1,2},{2,3},{4,5},{5,6},{6,7},{8,9},{9,10},{10,11},{12,13},{... | collective-permute-start | bytes 110600
  757.9 17.5 %collective-permute-start.7 = (bf16[18,1024]{1,0:T(8,128)(2,1)S(1)}, bf16[18,1024]{1,0:T(8,128)(2,1)S(1)}, u32[]{:S(2)}, u32[]{:S(2)}) collective-permute-start(bf16[18,1024]{1,0:T(8,128)(2,1)S(1)} %slice.95), channel_id=1, source_target_pairs={{0,1},{1,2},{2,3},{4,5},{5,6},{6,7},{8,9},{9,10},{10,11},{12,13},{... | collective-permute-start | bytes 110600
  867.3 5.5 copy-start.12
  867.3 5.4 copy-start.64
  868.9 12.2 collective-permute-start
  868.9 28.1 %collective-permute-start.1 = (bf16[146,1,1024]{2,0,1:T(8,128)(2,1)S(1)}, bf16[146,1,1024]{2,0,1:T(8,128)(2,1)}, u32[]{:S(2)}, u32[]{:S(2)}) collective-permute-start(bf16[146,1,1024]{2,0,1:T(8,128)(2,1)S(1)} %get-tuple-element.118), channel_id=1, source_target_pairs={{0,3},{1,0},{2,1},{3,2},{4,7},{5,4},{6,5},{7,6},{8,11},{9,8},{10,9... | collective-permute-start | bytes 897032 | tf_op jit(solution)/shard_map/ppermute | solution.py:36
  872.7 18.4 %copy-start.62 = (f32[146]{0:T(256)}, f32[146]{0:T(256)S(1)}, u32[]{:S(2)}) copy-start(f32[146]{0:T(256)S(1)} %negate_multiply_fusion.3) | copy-start | bytes 1756
  874.2 20.2 %collective-permute-start.3 = (bf16[146,1,1024]{2,0,1:T(8,128)(2,1)}, bf16[146,1,1024]{2,0,1:T(8,128)(2,1)}, u32[]{:S(2)}, u32[]{:S(2)}) collective-permute-start(bf16[146,1,1024]{2,0,1:T(8,128)(2,1)} %get-tuple-element.116), channel_id=1, source_target_pairs={{0,1},{1,2},{2,3},{3,0},{4,5},{5,6},{6,7},{7,4},{8,9},{9,10},{10,1... | collective-permute-start | bytes 897032 | tf_op jit(solution)/shard_map/ppermute | solution.py:28
  874.2 26.7 %collective-permute-start.4 = (bf16[146,1,1024]{2,0,1:T(8,128)(2,1)}, bf16[146,1,1024]{2,0,1:T(8,128)(2,1)}, u32[]{:S(2)}, u32[]{:S(2)}) collective-permute-start(bf16[146,1,1024]{2,0,1:T(8,128)(2,1)} %get-tuple-element.116), channel_id=1, source_target_pairs={{0,3},{1,0},{2,1},{3,2},{4,7},{5,4},{6,5},{7,6},{8,11},{9,8},{10,9... | collective-permute-start | bytes 897032 | tf_op jit(solution)/shard_map/ppermute | solution.py:36
  881.0 27.1 %collective-permute-start.2 = (bf16[146,1,1024]{2,0,1:T(8,128)(2,1)}, bf16[146,1,1024]{2,0,1:T(8,128)(2,1)}, u32[]{:S(2)}, u32[]{:S(2)}) collective-permute-start(bf16[146,1,1024]{2,0,1:T(8,128)(2,1)} %collective-permute-done), channel_id=1, source_target_pairs={{0,1},{1,2},{2,3},{3,0},{4,5},{5,6},{6,7},{7,4},{8,9},{9,10},{10,1... | collective-permute-start | bytes 897032 | tf_op jit(solution)/shard_map/ppermute | solution.py:28
  898.0 21.9 %slice-start.2 = ((s8[5980160]{0:T(1024)(128)(4,1)}), s8[1785856]{0:T(1024)(128)(4,1)S(1)}, s32[]{:S(2)}) async-start(s8[5980160]{0:T(1024)(128)(4,1)} %bitcast.223), calls=%async_computation.22 | async-start | bytes 3571712
  903.7 23.5 %collective-permute-start.5 = (bf16[146,1,1024]{2,0,1:T(8,128)(2,1)}, bf16[146,1,1024]{2,0,1:T(8,128)(2,1)}, u32[]{:S(2)}, u32[]{:S(2)}) collective-permute-start(bf16[146,1,1024]{2,0,1:T(8,128)(2,1)} %collective-permute-done.3), channel_id=1, source_target_pairs={{0,1},{1,2},{2,3},{3,0},{4,5},{5,6},{6,7},{7,4},{8,9},{9,10},{10,1... | collective-permute-start | bytes 897032 | tf_op jit(solution)/shard_map/ppermute | solution.py:28
  915.3 4.5 slice-start.3
  915.3 4.6 copy-start.18
  932.9 4.7 slice-start.1
  943.7 4.8 copy-start.29
  956.7 223.1 %all-reduce.26.cloned.1.call-start = ((), (), s32[]{:S(2)}) async-start(), calls=%async_computation.17 | async-start | bytes 9568256
  968.8 265.2 %reduce-scatter.15.cloned.1.call-start = ((), (), s32[]{:S(2)}) async-start(), calls=%async_computation.15 | async-start | bytes 4718592 | tf_op jit(solution)/shard_map/reduce_scatter | solution.py:273
  977.1 312.4 %reduce-scatter.17.cloned.1.call-start = ((), (), s32[]{:S(2)}) async-start(), calls=%async_computation.16 | async-start | bytes 4718592 | tf_op jit(solution)/shard_map/reduce_scatter | solution.py:274
  977.4 4.6 copy-start.38
  977.4 4.6 copy-start.43
  986.1 4.5 copy-start.70
  986.1 4.8 copy-start.33
  986.2 343.0 %reduce-scatter.13.cloned.1.call-start = ((), (), s32[]{:S(2)}) async-start(), calls=%async_computation.14 | async-start | bytes 1179648 | tf_op jit(solution)/shard_map/reduce_scatter | solution.py:272
  993.8 189.6 %copy-start.5 = (bf16[146,1,1024]{2,0,1:T(8,128)(2,1)S(1)}, bf16[146,1,1024]{2,0,1:T(8,128)(2,1)}, u32[]{:S(2)}) copy-start(bf16[146,1,1024]{2,0,1:T(8,128)(2,1)} %copy-done.4) | copy-start | bytes 897028
  993.8 189.7 %copy-start.45 = (f32[8,1,128]{2,1,0:T(1,128)S(1)}, f32[8,1,128]{2,1,0:T(1,128)}, u32[]{:S(2)}) copy-start(f32[8,1,128]{2,1,0:T(1,128)} %copy-done.44) | copy-start | bytes 12292
  993.8 189.7 %copy-start.50 = (f32[146]{0:T(256)S(1)}, f32[146]{0:T(256)}, u32[]{:S(2)}) copy-start(f32[146]{0:T(256)} %copy-done.49) | copy-start | bytes 1756
  993.8 189.9 %copy-start.69 = (f32[146]{0:T(256)S(1)}, f32[146]{0:T(256)}, u32[]{:S(2)}) copy-start(f32[146]{0:T(256)} %copy-done.68) | copy-start | bytes 1756
  993.8 190.0 %copy-start.3 = (bf16[146,1,1024]{2,0,1:T(8,128)(2,1)S(1)}, bf16[146,1,1024]{2,0,1:T(8,128)(2,1)}, u32[]{:S(2)}) copy-start(bf16[146,1,1024]{2,0,1:T(8,128)(2,1)} %copy-done.2) | copy-start | bytes 897028
  993.8 190.0 %copy-start.48 = (f32[146]{0:T(256)S(1)}, f32[146]{0:T(256)}, u32[]{:S(2)}) copy-start(f32[146]{0:T(256)} %copy-done.47) | copy-start | bytes 1756
  993.8 190.0 %copy-start.54 = (f32[146]{0:T(256)S(1)}, f32[146]{0:T(256)}, u32[]{:S(2)}) copy-start(f32[146]{0:T(256)} %copy-done.53) | copy-start | bytes 1756
  1183.8 27.4 %copy-start.13 = (f32[146,1,1024]{2,0,1:T(8,128)S(1)}, f32[146,1,1024]{2,0,1:T(8,128)}, u32[]{:S(2)}) copy-start(f32[146,1,1024]{2,0,1:T(8,128)} %copy-done.12) | copy-start | bytes 1794052
  1183.8 27.4 %copy-start.63 = (f32[146]{0:T(256)S(1)}, f32[146]{0:T(256)}, u32[]{:S(2)}) copy-start(f32[146]{0:T(256)} %copy-done.62) | copy-start | bytes 1756
  (53 other events, 157.5 us)
Sparse Core Ops, SparseCore 0:
  32.2 51.3 all-gather.15
  85.5 24.4 all-gather.17
  112.2 51.0 all-gather.25
  192.8 173.2 all-reduce.29
  368.0 26.8 all-gather.21
  397.0 51.0 all-gather.27
  450.3 49.8 all-gather.19
  501.8 49.8 all-gather.29
  553.7 26.9 all-gather.23
  582.2 51.0 all-gather.31
  646.4 214.8 all-reduce.27
  956.8 45.9 reduce-scatter.10
  1005.4 174.4 all-reduce.25
  1183.6 50.3 reduce-scatter.14
  1238.1 51.3 reduce-scatter.16
  1293.1 35.9 reduce-scatter.12
